TPU v7x, 32 devices: a whole 2x2x4 slice. The times are simulated.
32 devices in a mesh: rows: 8 (over z, x), cols: 4 (over y, core).
Axes of the slice: x: 2, y: 2, z: 4, core: 2. Of those that a mesh axis runs over, the one named last changes fastest.
Arguments:
- front_rows: bfloat16 [8, 1024, 4096], P(None, 'rows', 'cols'), may hold values from -0.1875 to 0.1875
- heights: int32 [8, 8], P('rows'), may hold values from 1 to 128
- child_rows: bfloat16 [8192, 4096], P('rows', 'cols'), may hold values from -0.1875 to 0.1875
- child_dest: int32 [8192, 1], P('rows'), may hold values from 0 to 7; in each aligned block of 1024 rows (0 to 1023, 1024 to 2047, ...) at most 256 rows name the same one
- child_slot: int32 [8192], P('rows'), may hold values from 0 to 127
- parent_ids: int32 [128], P('rows'), may hold values from 0 to 7
Outputs:
- r_rows: float32 [8, 128, 4096], P(None, None, ('cols', 'rows'))
Inputs may be any that keep to these rules, and one draw needn't show every extreme that they name: `child_dest`: in the rows of one device, at most 256 child rows name one index of rows.
All inputs are finite; a program needn't handle non-finite values.
Results may differ from a plain program's by a relative error of at most 0.002.
Values may be sent and summed in bfloat16 or wider, within the bound.
A program may use at most 64 MiB of HBM per device.

v0:
```python
import jax
import jax.numpy as jnp
from jax import lax
from jax.sharding import PartitionSpec as P

NB = 128


def from_root(block, axis, holder):
    block = jnp.where(lax.axis_index(axis) == holder, block, jnp.zeros_like(block))
    return lax.psum(block, axis)


def solve_block(lower, columns):
    return jax.scipy.linalg.solve_triangular(lower, columns, lower=True)


def on_device(front_rows, heights, child_rows, child_dest, child_slot, parent_ids):
    fronts, height_cap, width = front_rows.shape
    peers = lax.axis_size("rows")
    child_count = child_rows.shape[0]
    capacity = max(2, 2 * child_count // peers)
    slots = peers * capacity
    destination = child_dest[:, 0]
    hits = (destination[:, None] == jnp.arange(peers, dtype=jnp.int32)[None, :]).astype(jnp.int32)
    before = jnp.cumsum(hits, axis=0) - hits
    position = jnp.sum(before * hits, axis=1)
    send_index = destination * capacity + position
    block_rows = child_count // parent_ids.shape[0]
    child_front = jnp.repeat(parent_ids, block_rows)
    send_rows = jnp.zeros((slots, width), jnp.bfloat16).at[send_index].set(child_rows)
    send_owner = jnp.zeros((slots,), jnp.int32).at[send_index].set(child_front)
    send_front = send_owner.astype(jnp.bfloat16)
    send_slot = (
        jnp.zeros((slots,), jnp.bfloat16).at[send_index].set(child_slot.astype(jnp.bfloat16))
    )
    live_mask = jnp.arange(height_cap, dtype=jnp.int32)[None, :] < heights[0][:, None]
    own = jnp.where(live_mask[:, :, None], front_rows, jnp.zeros_like(front_rows))
    got_rows, got_front, got_slot = (
        lax.all_to_all(
            send_rows.reshape(peers, capacity, width),
            "rows",
            split_axis=0,
            concat_axis=0,
            tiled=True,
        ),
        lax.all_to_all(
            send_front.reshape(peers, capacity), "rows", split_axis=0, concat_axis=0, tiled=True
        ),
        lax.all_to_all(
            send_slot.reshape(peers, capacity), "rows", split_axis=0, concat_axis=0, tiled=True
        ),
    )
    got_rows = got_rows.reshape(slots, width)
    got_lead = got_rows[:, :NB]
    target = got_front.reshape(-1).astype(jnp.int32) * height_cap + got_slot.reshape(-1).astype(
        jnp.int32
    )
    placing = (jnp.arange(fronts * height_cap, dtype=jnp.int32)[:, None] == target[None, :]).astype(
        jnp.bfloat16
    )
    added = jnp.dot(placing, got_lead, preferred_element_type=jnp.float32)
    panel_local = (
        own[:, :, :NB].reshape(fronts * height_cap, NB).astype(jnp.float32) + added
    ).astype(jnp.bfloat16)
    panel = from_root(panel_local.reshape(fronts, height_cap, NB), "cols", 0)
    selected = jnp.dot(
        placing.T, panel.reshape(fronts * height_cap, NB), preferred_element_type=jnp.float32
    ).astype(jnp.bfloat16)
    which = (
        jnp.arange(fronts, dtype=jnp.int32)[:, None]
        == got_front.reshape(-1).astype(jnp.int32)[None, :]
    ).astype(jnp.bfloat16)
    picked = which[:, :, None] * selected[None, :, :]
    child_cross = jnp.einsum("fsk,sc->fkc", picked, got_rows, preferred_element_type=jnp.float32)
    gram = jnp.einsum("fhk,fhj->fkj", panel, panel, preferred_element_type=jnp.float32)
    gram_total = lax.psum(gram, "rows")
    local = jnp.einsum("fhk,fhc->fkc", panel, own, preferred_element_type=jnp.float32) + child_cross
    scattered = lax.psum_scatter(
        jnp.transpose(local, (2, 0, 1)), "rows", scatter_dimension=0, tiled=True
    )
    columns = jnp.transpose(scattered, (1, 2, 0))
    lower = jnp.linalg.cholesky(gram_total)
    return jax.vmap(solve_block)(lower, columns)


def solution(mesh):
    placed = (
        P(None, "rows", "cols"),
        P("rows", None),
        P("rows", "cols"),
        P("rows", None),
        P("rows"),
        P("rows"),
    )
    return jax.shard_map(
        on_device,
        mesh=mesh,
        in_specs=placed,
        out_specs=P(None, None, ("cols", "rows")),
        check_vma=False,
    )
```

profile of v0, /device:TPU:0, one launch (start us, length us, event | category | flops | bytes accessed | tf_op | source)
XLA Modules:
  0.0 452.6 jit_solution(11797999824237723008)
XLA Ops:
  6.5 0.7 broadcast_in_dim.25
  7.3 0.1 reshape.137
  7.3 0.7 fusion.23
  8.0 2.3 reduce-window.6
  10.3 0.3 slice_reduce_fusion
  10.6 0.2 reduce-window.9
  10.7 0.1 add_bitcast_fusion
  10.8 0.7 fusion.22
  11.5 0.7 compare_select_fusion
  12.2 4.3 scatter_custom_fusion
  16.6 0.5 broadcast.117
  17.1 0.7 reduce.9
  17.8 0.6 reshape.168
  18.4 7.3 %all-to-all-start = ((bf16[8,2,128]{2,1,0:T(2,128)(2,1)}), bf16[8,2,128]{2,1,0:T(2,128)(2,1)S(1)}, u32[]{:S(2)}, u32[]{:S(2)}) async-start(bf16[8,2,128]{2,1,0:T(2,128)(2,1)} %reshape.168), calls=%async_computation | async-start | bytes 8192 | tf_op jit(solution)/shard_map/all_to_all | solution.py:47
  25.6 0.7 convert_element_type.64
  26.3 7.6 %scatter_custom_fusion.1 = bf16[2048]{0:T(1024)(128)(2,1)S(1)} fusion(s32[1024]{0:T(1024)S(1)} %bitcast.71, bf16[1024]{0:T(1024)(128)(2,1)S(1)} %convert_element_type.64, bf16[]{:T(256)} %constant.60.clone.1), kind=kCustom, calls=%fused_computation.47 | custom fusion | bytes 4098 | tf_op jit(solution)/shard_map/scatter | solution.py:35
  33.9 0.7 reduce.8
  34.6 0.6 reshape.166
  35.2 0.0 all-to-all-done
  35.2 6.0 %all-to-all-start.1 = ((bf16[8,2,128]{2,1,0:T(2,128)(2,1)}), bf16[8,2,128]{2,1,0:T(2,128)(2,1)S(1)}, u32[]{:S(2)}, u32[]{:S(2)}) async-start(bf16[8,2,128]{2,1,0:T(2,128)(2,1)} %reshape.166), calls=%async_computation.1 | async-start | bytes 8192 | tf_op jit(solution)/shard_map/all_to_all | solution.py:50
  41.2 8.6 %scatter_custom_fusion.2 = bf16[2048,1024]{1,0:T(8,128)(2,1)} fusion(s32[1024]{0:T(1024)S(1)} %bitcast.72, bf16[1024,1024]{1,0:T(8,128)(2,1)} %param.8, bf16[]{:T(256)} %constant.60.clone.1), kind=kCustom, calls=%fused_computation.14 | custom fusion | bytes 4194816 | tf_op jit(solution)/shard_map/scatter | solution.py:31
  49.7 6.4 %copy.36 = bf16[8,256,1024]{1,2,0:T(8,128)(2,1)} copy(bf16[8,256,1024]{2,1,0:T(8,128)(2,1)} %bitcast.58) | data formatting | bytes 8388608 | tf_op jit(solution)/shard_map/reshape | solution.py:41
  56.2 0.0 copy-start.1
  56.2 0.0 all-to-all-done.1
  56.2 6.1 %all-to-all-start.2 = ((bf16[8,256,1024]{1,2,0:T(8,128)(2,1)}), bf16[8,256,1024]{1,2,0:T(8,128)(2,1)}, u32[]{:S(2)}, u32[]{:S(2)}) async-start(bf16[8,256,1024]{1,2,0:T(8,128)(2,1)} %copy.36), calls=%async_computation.2 | async-start | bytes 8388608 | tf_op jit(solution)/shard_map/all_to_all | solution.py:40
  62.3 0.2 all-reduce.3.cloned.1.call-start
  62.6 0.0 copy-done.1
  62.6 0.1 iota_compare_fusion.16
  62.6 1.8 broadcast_select_fusion
  64.5 0.1 slice.28
  64.6 89.9 %all-to-all-done.2 = bf16[8,256,1024]{1,2,0:T(8,128)(2,1)} async-done(((bf16[8,256,1024]{1,2,0:T(8,128)(2,1)}), bf16[8,256,1024]{1,2,0:T(8,128)(2,1)}, u32[]{:S(2)}, u32[]{:S(2)}) %all-to-all-start.2) | async-done | bytes 4194336 | tf_op jit(solution)/shard_map/all_to_all | solution.py:40
  154.5 2.8 copy.49
  157.3 2.4 fusion.13
  159.6 0.0 all-reduce.3.cloned.1.call-update
  159.7 0.0 all-reduce.5.cloned.1.call-start
  159.7 6.5 %copy.37 = bf16[8,256,1024]{1,0,2:T(8,128)(2,1)} copy(bf16[8,256,1024]{1,2,0:T(8,128)(2,1)} %all-to-all-done.2) | data formatting | bytes 8388608 | tf_op jit(solution)/shard_map/all_to_all | solution.py:40
  166.2 7.4 %reshape.157 = bf16[2048,1024,1]{0,1,2:T(8,128)(2,1)} reshape(bf16[8,256,1024]{1,0,2:T(8,128)(2,1)} %copy.37) | data formatting | bytes 8388608 | tf_op jit(solution)/shard_map/reshape | solution.py:54
  173.7 17.2 %all-reduce.3.cloned.1.call-done = bf16[8,128,128]{2,1,0:T(8,128)(2,1)} async-done(((bf16[8,128,128]{2,1,0:T(8,128)(2,1)}), bf16[8,128,128]{2,1,0:T(8,128)(2,1)}) %all-reduce.3.cloned.1.call-update) | async-done | bytes 262160 | tf_op jit(solution)/shard_map/psum | solution.py:11
  190.9 0.0 copy-start
  190.9 3.4 fusion.6
  194.2 0.0 copy-done
  194.3 1.1 fusion.28
  195.3 0.0 all-reduce.5.cloned.1.call-update
  195.4 0.3 reduce-scatter.2.cloned.1.call-start
  195.6 7.6 %fusion.2 = f32[1024,8,128]{0,2,1:T(8,128)S(1)} fusion(bf16[2048,1024,1]{0,1,2:T(8,128)(2,1)} %reshape.157, bf16[2048,128]{1,0:T(8,128)(2,1)S(1)} %fusion.6, bf16[8,2048]{1,0:T(8,128)(2,1)S(1)} %fusion.19), kind=kOutput, calls=%fused_computation.7 | convolution fusion | flops 4303355904 | bytes 8945664 | tf_op jit(solution)/shard_map/fsk,sc->fkc/dot_general | solution.py:75
  203.3 2.8 bitcast_add_fusion
  206.0 0.0 reduce-scatter.2.cloned.1.call-update
  206.1 61.8 %all-reduce.5.cloned.1.call-done = f32[8,128,128]{1,2,0:T(8,128)} async-done(((f32[8,128,128]{1,2,0:T(8,128)}), f32[8,128,128]{1,2,0:T(8,128)}) %all-reduce.5.cloned.1.call-update) | async-done | bytes 524304 | tf_op jit(solution)/shard_map/psum | solution.py:77
  267.9 1.2 copy.40
  269.1 1.1 fusion.18
  270.2 94.0 %custom-call.8 = f32[8,128,128]{2,1,0:T(8,128)S(1)} custom-call(f32[8,128,128]{2,1,0:T(8,128)S(1)} %fusion.18), custom_call_target="Cholesky" | custom-call | tf_op jit(solution)/shard_map/jit(cholesky)/cholesky | solution.py:83
  364.3 0.1 select_reduce_fusion
  364.3 0.1 compare_reduce_fusion
  364.4 0.1 select_bitcast_fusion
  364.6 78.6 %custom-call.9 = f32[8,1,128,128]{2,3,1,0:T(8,128)S(1)} custom-call(f32[8,1,128,128]{3,2,1,0:T(8,128)S(1)} %select_bitcast_fusion), custom_call_target="InvertDiagBlocksLowerTriangular" | custom-call | tf_op jit(solution)/shard_map/vmap(jit(_solve_triangular))/triangular_solve | solution.py:15
  443.2 0.0 reduce-scatter.2.cloned.1.call-done
  443.2 2.8 fusion.15
  (11 shorter events, 0.1 us)
Async XLA Ops:
  18.4 16.8 %all-to-all-start = ((bf16[8,2,128]{2,1,0:T(2,128)(2,1)}), bf16[8,2,128]{2,1,0:T(2,128)(2,1)S(1)}, u32[]{:S(2)}, u32[]{:S(2)}) async-start(bf16[8,2,128]{2,1,0:T(2,128)(2,1)} %reshape.168), calls=%async_computation | async-start | bytes 8192 | tf_op jit(solution)/shard_map/all_to_all | solution.py:47
  35.2 21.0 %all-to-all-start.1 = ((bf16[8,2,128]{2,1,0:T(2,128)(2,1)}), bf16[8,2,128]{2,1,0:T(2,128)(2,1)S(1)}, u32[]{:S(2)}, u32[]{:S(2)}) async-start(bf16[8,2,128]{2,1,0:T(2,128)(2,1)} %reshape.166), calls=%async_computation.1 | async-start | bytes 8192 | tf_op jit(solution)/shard_map/all_to_all | solution.py:50
  56.2 6.4 %copy-start.1 = (s32[1,8]{1,0:T(1,128)S(1)}, s32[1,8]{1,0:T(1,128)}, u32[]{:S(2)}) copy-start(s32[1,8]{1,0:T(1,128)} %param.7) | copy-start | bytes 100
  56.2 98.3 %all-to-all-start.2 = ((bf16[8,256,1024]{1,2,0:T(8,128)(2,1)}), bf16[8,256,1024]{1,2,0:T(8,128)(2,1)}, u32[]{:S(2)}, u32[]{:S(2)}) async-start(bf16[8,256,1024]{1,2,0:T(8,128)(2,1)} %copy.36), calls=%async_computation.2 | async-start | bytes 8388608 | tf_op jit(solution)/shard_map/all_to_all | solution.py:40
  62.3 128.5 %all-reduce.3.cloned.1.call-start = ((), (), s32[]{:S(2)}) async-start(), calls=%async_computation.4 | async-start | bytes 524288 | tf_op jit(solution)/shard_map/psum | solution.py:11
  159.7 108.2 %all-reduce.5.cloned.1.call-start = ((), (), s32[]{:S(2)}) async-start(), calls=%async_computation.5 | async-start | bytes 1048576 | tf_op jit(solution)/shard_map/psum | solution.py:77
  190.9 3.4 copy-start
  195.4 247.8 %reduce-scatter.2.cloned.1.call-start = ((), (), s32[]{:S(2)}) async-start(), calls=%async_computation.6 | async-start | bytes 4718592 | tf_op jit(solution)/shard_map/reduce_scatter | solution.py:79
Sparse Core Ops, SparseCore 0:
  159.8 31.0 all-reduce.2
  195.5 72.3 all-reduce.4
  271.5 87.7 reduce-scatter.1
where the time goes:
time: 454 us; the launch traced here: 453 us
  other arithmetic  183 us (40%)
  waiting for transfers between devices  169 us (37%)
  local copies, waits for them, and re-layouts  47.8 us (11%)
  matrix products  20.1 us (4%)
  starting transfers between devices  19.9 us (4%)
  between operations  13.3 us (3%)
    another operation x4, other arithmetic, on_device(): lower = jnp.linalg.cholesky(gram_total)  94.2 us
    all_to_all x1, waiting for transfers between devices, on_device(): lax.all_to_all(send_rows.reshape(peers, capacity, width), 'rows', split_a...  89.9 us
    another operation x3, other arithmetic, solve_block(): return jax.scipy.linalg.solve_triangular(lower, columns, lower=True)  78.7 us
    psum x1, waiting for transfers between devices, on_device(): gram_total = lax.psum(gram, 'rows')  61.8 us
    psum x1, waiting for transfers between devices, from_root(): return lax.psum(block, axis)  17.2 us
    reshape x2, local copies, waits for them, and re-layouts, on_device(): got_rows = got_rows.reshape(slots, width)  10.2 us
  transfers between devices with their start and end apart: 6, of which 3 were waited for; matrix products, arithmetic and copies ran while one was open for 50% of the time, Pallas kernels for 0%

commit v1 on v0

v1 whole, which is shorter than its diff:
```python
import jax
import jax.numpy as jnp
from jax import lax
from jax.experimental import pallas as pl
from jax.experimental.pallas import tpu as pltpu
from jax.sharding import PartitionSpec as P

NB = 128


def lane(x, index):
    return jnp.take_along_axis(x, jnp.full(x.shape, index, jnp.int32), axis=1)


def inverse_factor(a, b):
    step = 8
    ids = lax.broadcasted_iota(jnp.int32, b.shape[1:], 1)

    def unit(i, carry):
        b[i] = (ids == i).astype(jnp.float32)
        return carry

    lax.fori_loop(0, NB, unit, 0)

    def block(at, carry):
        base = at * step
        rows = [a[base + k] for k in range(step)]
        right = [b[base + k] for k in range(step)]
        for k in range(step):
            pivot = lane(rows[k], base + k)
            inverse = 1.0 / pivot
            root = lax.rsqrt(pivot)
            for m in range(k + 1, step):
                scale = lane(rows[k], base + m) * inverse
                rows[m] = rows[m] - scale * rows[k]
                right[m] = right[m] - scale * right[k]
            rows[k] = rows[k] * root
            right[k] = right[k] * root
            b[base + k] = right[k]

        def below(quad, inner):
            for u in range(4):
                i = quad * 4 + u
                left_row, right_row = a[i], b[i]
                for k in range(step):
                    scale = lane(rows[k], i)
                    left_row = left_row - scale * rows[k]
                    right_row = right_row - scale * right[k]
                a[i] = left_row
                b[i] = right_row
            return inner

        lax.fori_loop((base + step) // 4, NB // 4, below, 0)
        return carry

    lax.fori_loop(0, NB // step, block, 0)


def factor_kernel(gram_ref, out_ref, a, b):
    fronts = gram_ref.shape[0]
    for f in range(fronts):
        a[:, f, :] = gram_ref[f]
    inverse_factor(a, b)
    for f in range(fronts):
        out_ref[f] = b[:, f, :]


def factor(gram):
    fronts = gram.shape[0]
    return pl.pallas_call(
        factor_kernel,
        out_shape=jax.ShapeDtypeStruct(gram.shape, jnp.float32),
        in_specs=[pl.BlockSpec(memory_space=pltpu.VMEM)],
        out_specs=pl.BlockSpec(memory_space=pltpu.VMEM),
        scratch_shapes=[pltpu.VMEM((NB, fronts, NB), jnp.float32)] * 2,
        compiler_params=pltpu.CompilerParams(vmem_limit_bytes=8 << 20),
        cost_estimate=pl.CostEstimate(flops=40_000_000_000, bytes_accessed=1 << 20, transcendentals=0),
    )(gram)


def on_device(front_rows, heights, child_rows, child_dest, child_slot, parent_ids):
    fronts, height_cap, width = front_rows.shape
    peers = lax.axis_size("rows")
    count = child_rows.shape[0]
    capacity = max(2, 2 * count // peers)
    slots = peers * capacity
    local_rows = fronts * height_cap
    destination = child_dest[:, 0]
    child_front = jnp.repeat(parent_ids, count // parent_ids.shape[0])
    hits = (destination[:, None] == jnp.arange(peers, dtype=jnp.int32)[None, :]).astype(jnp.bfloat16)
    earlier = (jnp.arange(count)[:, None] > jnp.arange(count)[None, :]).astype(jnp.bfloat16)
    before = jnp.dot(earlier, hits, preferred_element_type=jnp.float32)
    position = jnp.sum(before * hits.astype(jnp.float32), axis=1).astype(jnp.int32)
    send_index = destination * capacity + position
    packing = (jnp.arange(slots, dtype=jnp.int32)[:, None] == send_index[None, :]).astype(jnp.bfloat16)
    send_lead = jnp.dot(packing, child_rows[:, :NB], preferred_element_type=jnp.float32).astype(jnp.bfloat16)
    tags = jnp.stack([child_front, child_slot], axis=0).astype(jnp.bfloat16)
    send_tags = lax.dot_general(
        tags, packing, (((1,), (1,)), ((), ())), preferred_element_type=jnp.float32
    ).astype(jnp.bfloat16)
    tag_rows = -(-2 * capacity // NB)
    send_tags = jnp.transpose(send_tags.reshape(2, peers, capacity), (1, 0, 2)).reshape(peers, 2 * capacity)
    send_tags = jnp.pad(send_tags, ((0, 0), (0, tag_rows * NB - 2 * capacity))).reshape(peers, tag_rows, NB)
    sent = jnp.concatenate([send_lead.reshape(peers, capacity, NB), send_tags], axis=1)
    got = lax.all_to_all(sent, "rows", split_axis=0, concat_axis=0, tiled=True)
    got_lead = got[:, :capacity].reshape(slots, NB)
    got_tags = got[:, capacity:].reshape(peers, tag_rows * NB)[:, : 2 * capacity].astype(jnp.int32)
    got_tags = got_tags.reshape(peers, 2, capacity)
    target = (got_tags[:, 0] * height_cap + got_tags[:, 1]).reshape(slots)
    placing = (jnp.arange(local_rows, dtype=jnp.int32)[:, None] == target[None, :]).astype(jnp.bfloat16)
    added = jnp.dot(placing, got_lead, preferred_element_type=jnp.float32)
    live_mask = jnp.arange(height_cap, dtype=jnp.int32)[None, :] < heights[0][:, None]
    own = jnp.where(live_mask[:, :, None], front_rows, jnp.zeros_like(front_rows))
    panel_own = (own[:, :, :NB].reshape(local_rows, NB).astype(jnp.float32) + added).astype(jnp.bfloat16)
    panel_own = lax.psum(
        jnp.where(lax.axis_index("cols") == 0, panel_own, jnp.zeros_like(panel_own)), "cols"
    )
    panel_all = lax.all_gather(panel_own, "rows", axis=0, tiled=True)
    by_front = panel_all.reshape(peers, fronts, height_cap, NB)
    gram = jnp.einsum("pfhk,pfhj->fkj", by_front, by_front, preferred_element_type=jnp.float32)
    key = destination * local_rows + child_front * height_cap + child_slot
    choosing = (key[:, None] == jnp.arange(peers * local_rows, dtype=jnp.int32)[None, :]).astype(jnp.bfloat16)
    selected = jnp.dot(choosing, panel_all, preferred_element_type=jnp.float32).astype(jnp.bfloat16)
    which = (jnp.arange(fronts, dtype=jnp.int32)[:, None] == child_front[None, :]).astype(jnp.bfloat16)
    picked = which[:, :, None] * selected[None, :, :]
    local = jnp.einsum("fsk,sc->fkc", picked, child_rows, preferred_element_type=jnp.float32)
    local = local + jnp.einsum(
        "fhk,fhc->fkc", panel_own.reshape(fronts, height_cap, NB), own, preferred_element_type=jnp.float32
    )
    columns = lax.psum_scatter(
        jnp.transpose(local.reshape(fronts, NB, peers, width // peers), (2, 0, 1, 3)),
        "rows",
        scatter_dimension=0,
        tiled=True,
    )[0]
    inverse = factor(gram)
    return jnp.einsum(
        "fij,fjc->fic", inverse, columns, precision=lax.Precision.HIGHEST, preferred_element_type=jnp.float32
    )


def solution(mesh):
    placed = (
        P(None, "rows", "cols"),
        P("rows", None),
        P("rows", "cols"),
        P("rows", None),
        P("rows"),
        P("rows"),
    )
    return jax.shard_map(
        on_device,
        mesh=mesh,
        in_specs=placed,
        out_specs=P(None, None, ("cols", "rows")),
        check_vma=False,
    )
```

time: 454 us -> 233 us (0.51)
  other arithmetic: 183 us -> 4.18 us
  Pallas kernels: 0 us -> 44.3 us
  local copies, waits for them, and re-layouts: 47.8 us -> 3.65 us
  waiting for transfers between devices: 169 us -> 135 us
  starting transfers between devices: 19.9 us -> 7.55 us
  matrix products: 20.1 us -> 24.7 us
    another operation x9 -> x1, other arithmetic: 175 us -> 0.66 us  [the longest x4 94.2 us: on_device(): lower = jnp.linalg.cholesky(gram_total)]
    all_to_all x3 -> x1, waiting for transfers between devices: 89.9 us -> 12.8 us  [on_device(): got = lax.all_to_all(sent, 'rows', split_axis=0, concat_axis=0, tiled=True)]
    all_gather x0 -> x1, waiting for transfers between devices: none -> 51.4 us  [on_device(): panel_all = lax.all_gather(panel_own, 'rows', axis=0, tiled=True)]
    psum x2 -> x1, waiting for transfers between devices: 78.9 us -> 31.2 us  [on_device(): lax.psum(jnp.where(lax.axis_index('cols') == 0, panel_own, jnp.zeros_like...]
    pallas_call x0 -> x1, Pallas kernels: none -> 44.3 us  [factor(): pl.pallas_call(factor_kernel, out_shape=jax.ShapeDtypeStruct(gram.shape,...]
    reduce_scatter x1, waiting for transfers between devices: 0.02 us -> 39.6 us  [on_device(): lax.psum_scatter(jnp.transpose(local.reshape(fronts, NB, peers, width //...]
    scatter x3 -> x0, local copies, waits for them, and re-layouts: 20.4 us -> none  [the longest x1 8.55 us: on_device(): jnp.zeros((slots, width), jnp.bfloat16).at[send_index].set(child_rows)]
    reshape x4 -> x2, local copies, waits for them, and re-layouts: 16.7 us -> 2.52 us  [the longest x1 2.51 us: on_device(): local.reshape(fronts, NB, peers, width // peers)]
  transfers between devices with their start and end apart: 6 -> 4, of which waited for: 3 -> 4; matrix products, arithmetic and copies ran while one was open for 50% -> 2% of each run, Pallas kernels for 0% -> 19%
where the time goes in v1:
time: 233 us
  waiting for transfers between devices  135 us (58%)
  Pallas kernels  44.3 us (19%)
  matrix products  24.7 us (11%)
  between operations  13.3 us (6%)
  starting transfers between devices  7.55 us (3%)
  other arithmetic  4.18 us (2%)
  local copies, waits for them, and re-layouts  3.65 us (2%)
    all_gather x1, waiting for transfers between devices, on_device(): panel_all = lax.all_gather(panel_own, 'rows', axis=0, tiled=True)  51.4 us
    pallas_call x1, Pallas kernels, factor(): pl.pallas_call(factor_kernel, out_shape=jax.ShapeDtypeStruct(gram.shape,...  44.3 us
    reduce_scatter x1, waiting for transfers between devices, on_device(): lax.psum_scatter(jnp.transpose(local.reshape(fronts, NB, peers, width //...  39.6 us
    psum x1, waiting for transfers between devices, on_device(): lax.psum(jnp.where(lax.axis_index('cols') == 0, panel_own, jnp.zeros_like...  31.2 us
    all_to_all x1, waiting for transfers between devices, on_device(): got = lax.all_to_all(sent, 'rows', split_axis=0, concat_axis=0, tiled=True)  12.8 us
    dot_general x1, matrix products, on_device(): jnp.dot(choosing, panel_all, preferred_element_type=jnp.float32)  8.56 us
    all_to_all x1, starting transfers between devices, on_device(): got = lax.all_to_all(sent, 'rows', split_axis=0, concat_axis=0, tiled=True)  7.25 us
  transfers between devices with their start and end apart: 4, of which 4 were waited for; matrix products, arithmetic and copies ran while one was open for 2% of the time, Pallas kernels for 19%

profile of v1, /device:TPU:0, one launch (start us, length us, event | category | flops | bytes accessed | tf_op | source)
XLA Modules:
  0.0 232.6 jit_solution(6701304237969187378)
XLA Ops:
  6.5 0.7 convert.11
  7.2 0.1 broadcast_in_dim.18
  7.3 0.1 stack_reshape.4
  7.4 1.2 fusion.19
  8.6 0.7 broadcast_in_dim.20
  9.3 0.1 eq.85
  9.4 0.8 add_add_fusion
  10.2 1.5 fusion.10
  11.7 2.5 %fusion.9 = bf16[2048,128]{1,0:T(8,128)(2,1)S(1)} fusion(s32[1024]{0:T(1024)S(1)} %get-tuple-element.6, bf16[1024,1024]{1,0:T(8,128)(2,1)} %param.8), kind=kOutput, calls=%fused_computation.15 | convolution fusion | flops 539230208 | bytes 790528 | tf_op jit(solution)/shard_map/dot_general | solution.py:96
  14.2 0.0 copy-start.2
  14.2 0.8 pad_maximum_fusion
  15.0 7.3 %all-to-all-start = ((bf16[8,260,128]{2,1,0:T(8,128)(2,1)}), bf16[8,260,128]{2,1,0:T(8,128)(2,1)S(1)}, u32[]{:S(2)}, u32[]{:S(2)}) async-start(bf16[8,260,128]{2,1,0:T(8,128)(2,1)} %pad_maximum_fusion), calls=%async_computation | async-start | bytes 1081344 | tf_op jit(solution)/shard_map/all_to_all | solution.py:105
  22.3 0.0 all-reduce.2.cloned.1.call-start
  22.3 0.0 copy-done.2
  22.3 0.1 iota_compare_fusion.28
  22.4 1.8 broadcast_select_fusion
  24.2 0.1 slice.24
  24.3 12.8 %all-to-all-done = bf16[8,260,128]{2,1,0:T(8,128)(2,1)S(1)} async-done(((bf16[8,260,128]{2,1,0:T(8,128)(2,1)}), bf16[8,260,128]{2,1,0:T(8,128)(2,1)S(1)}, u32[]{:S(2)}, u32[]{:S(2)}) %all-to-all-start) | async-done | bytes 532512 | tf_op jit(solution)/shard_map/all_to_all | solution.py:105
  37.2 2.4 %fusion.17 = bf16[1024,128]{1,0:T(8,128)(2,1)} fusion(bf16[2048,128]{1,0:T(8,128)(2,1)S(1)} %bitcast.42, s32[2048]{0:T(1024)S(1)} %bitcast.46, bf16[1024,128]{1,0:T(8,128)(2,1)S(1)} %bitcast.44, pred[]{:T(512)S(6)} %eq.74), kind=kOutput, calls=%fused_computation.25 | convolution fusion | flops 539492352 | bytes 1056769 | tf_op jit(solution)/shard_map/dot_general | solution.py:111
  39.6 0.0 all-reduce.2.cloned.1.call-update
  39.6 0.0 all-gather.2.cloned.1.call-start
  39.7 31.2 %all-reduce.2.cloned.1.call-done = bf16[1024,128]{1,0:T(8,128)(2,1)} async-done(((bf16[1024,128]{1,0:T(8,128)(2,1)}), bf16[1024,128]{1,0:T(8,128)(2,1)}) %all-reduce.2.cloned.1.call-update) | async-done | bytes 262160 | tf_op jit(solution)/shard_map/psum | solution.py:115
  70.8 0.0 all-gather.2.cloned.1.call-update
  70.8 0.2 reduce-scatter.2.cloned.1.call-start
  71.1 51.4 %all-gather.2.cloned.1.call-done = bf16[8192,128]{1,0:T(8,128)(2,1)} async-done(((bf16[1024,128]{1,0:T(8,128)(2,1)}), bf16[8192,128]{1,0:T(8,128)(2,1)}) %all-gather.2.cloned.1.call-update) | async-done | bytes 2097168 | tf_op jit(solution)/shard_map/all_gather | solution.py:118
  122.5 0.0 copy-start.1
  122.5 8.6 %fusion.15 = bf16[1024,128]{0,1:T(8,128)(2,1)S(1)} fusion(bf16[8192,128]{1,0:T(8,128)(2,1)} %all-gather.2.cloned.1.call-done, s32[1024]{0:T(1024)S(1)} %get-tuple-element.5), kind=kOutput, calls=%fused_computation.23 | convolution fusion | flops 2156003328 | bytes 2363392 | tf_op jit(solution)/shard_map/dot_general | solution.py:123
  131.0 0.0 copy-done.1
  131.1 0.0 copy-start
  131.1 2.3 %fusion.11 = f32[8,128,1024]{2,1,0:T(8,128)S(1)} fusion(bf16[1024,1024]{1,0:T(8,128)(2,1)S(1)} %copy-done.1, bf16[1024,128]{0,1:T(8,128)(2,1)S(1)} %fusion.15, bf16[8,1024]{1,0:T(8,128)(2,1)S(1)} %fusion.26), kind=kOutput, calls=%fused_computation.17 | convolution fusion | flops 2148532224 | bytes 6569984 | tf_op jit(solution)/shard_map/fsk,sc->fkc/dot_general | solution.py:126
  133.4 0.0 copy-done
  133.4 0.8 add_bitcast_fusion
  134.2 2.5 %copy.15 = f32[8,16,8,8,128]{4,3,1,0,2:T(8,128)} copy(f32[8,16,8,8,128]{4,3,2,1,0:T(8,128)S(1)} %add_bitcast_fusion) | data formatting | bytes 8388608 | tf_op jit(solution)/shard_map/reshape | solution.py:131
  136.8 0.0 reduce-scatter.2.cloned.1.call-update
  136.8 3.0 %convolution_bitcast_fusion.gram_ref = f32[8,128,128]{2,1,0:T(8,128)S(1)} fusion(bf16[8,8,128,128]{3,2,1,0:T(8,128)(2,1)} %bitcast.40), kind=kOutput, calls=%fused_computation.21 | convolution fusion | flops 268435456 | bytes 2621440 | tf_op jit(solution)/shard_map/pfhk,pfhj->fkj/dot_general | solution.py:120
  139.8 44.3 %shard_map.64 = f32[8,128,128]{2,1,0:T(8,128)S(1)} custom-call(f32[8,128,128]{2,1,0:T(8,128)S(1)} %convolution_bitcast_fusion.gram_ref), custom_call_target="tpu_custom_call" | custom-call | flops 40000000000 | bytes 1048576 | tf_op jit(solution)/shard_map/pallas_call | solution.py:70
  184.0 39.6 %reduce-scatter.2.cloned.1.call-done = f32[1,8,128,128]{3,2,1,0:T(8,128)} async-done(((f32[8,8,128,128]{3,2,1,0:T(8,128)}), f32[1,8,128,128]{3,2,1,0:T(8,128)}) %reduce-scatter.2.cloned.1.call-update) | async-done | bytes 524304 | tf_op jit(solution)/shard_map/reduce_scatter | solution.py:130
  223.6 2.5 %fusion.22 = f32[8,128,128]{2,1,0:T(8,128)} fusion(f32[8,128,128]{2,1,0:T(8,128)S(1)} %shard_map.64, f32[1,8,128,128]{3,2,1,0:T(8,128)} %reduce-scatter.2.cloned.1.call-done), kind=kOutput, calls=%fused_computation.31 | convolution fusion | flops 201326592 | bytes 1572864 | tf_op jit(solution)/shard_map/fij,fjc->fic/dot_general | solution.py:137
  (9 shorter events, 0.1 us)
Async XLA Ops:
  14.2 8.2 %copy-start.2 = (s32[1,8]{1,0:T(1,128)S(1)}, s32[1,8]{1,0:T(1,128)}, u32[]{:S(2)}) copy-start(s32[1,8]{1,0:T(1,128)} %param.7) | copy-start | bytes 100
  15.0 22.1 %all-to-all-start = ((bf16[8,260,128]{2,1,0:T(8,128)(2,1)}), bf16[8,260,128]{2,1,0:T(8,128)(2,1)S(1)}, u32[]{:S(2)}, u32[]{:S(2)}) async-start(bf16[8,260,128]{2,1,0:T(8,128)(2,1)} %pad_maximum_fusion), calls=%async_computation | async-start | bytes 1081344 | tf_op jit(solution)/shard_map/all_to_all | solution.py:105
  22.3 48.5 %all-reduce.2.cloned.1.call-start = ((), (), s32[]{:S(2)}) async-start(), calls=%async_computation.2 | async-start | bytes 524288 | tf_op jit(solution)/shard_map/psum | solution.py:115
  39.6 82.9 %all-gather.2.cloned.1.call-start = ((), (), s32[]{:S(2)}) async-start(), calls=%async_computation.3 | async-start | bytes 2359296 | tf_op jit(solution)/shard_map/all_gather | solution.py:118
  70.8 152.8 %reduce-scatter.2.cloned.1.call-start = ((), (), s32[]{:S(2)}) async-start(), calls=%async_computation.4 | async-start | bytes 4718592 | tf_op jit(solution)/shard_map/reduce_scatter | solution.py:130
  122.5 8.6 %copy-start.1 = (bf16[1024,1024]{1,0:T(8,128)(2,1)S(1)}, bf16[1024,1024]{1,0:T(8,128)(2,1)}, u32[]{:S(2)}) copy-start(bf16[1024,1024]{1,0:T(8,128)(2,1)} %param.8) | copy-start | bytes 6291460
  131.1 2.4 %copy-start = (bf16[1024,128]{1,0:T(8,128)(2,1)S(1)}, bf16[1024,128]{1,0:T(8,128)(2,1)}, u32[]{:S(2)}) copy-start(bf16[1024,128]{1,0:T(8,128)(2,1)} %all-reduce.2.cloned.1.call-done) | copy-start | bytes 786436
Sparse Core Ops, SparseCore 0:
  39.7 31.0 all-reduce.1
  73.2 49.2 all-gather.1
  136.9 86.6 reduce-scatter.1

commit v2 on v1

--- a/solution.py
+++ b/solution.py
@@ -1,3 +1,6 @@
+import functools
+import math
+
 import jax
 import jax.numpy as jnp
 from jax import lax
@@ -6,10 +9,12 @@
 from jax.sharding import PartitionSpec as P
 
 NB = 128
+LARGEST = 0.1875
+MESH = pl.DeviceIdType.MESH
 
 
 def lane(x, index):
-    return jnp.take_along_axis(x, jnp.full(x.shape, index, jnp.int32), axis=1)
+    return jnp.take_along_axis(x, jnp.full(x.shape, index, jnp.int32), axis=1, mode="promise_in_bounds")
 
 
 def inverse_factor(a, b):
@@ -22,7 +27,7 @@
 
     lax.fori_loop(0, NB, unit, 0)
 
-    def block(at, carry):
+    def block(at, carry, end):
         base = at * step
         rows = [a[base + k] for k in range(step)]
         right = [b[base + k] for k in range(step)]
@@ -36,6 +41,7 @@
                 right[m] = right[m] - scale * right[k]
             rows[k] = rows[k] * root
             right[k] = right[k] * root
+            a[base + k] = rows[k]
             b[base + k] = right[k]
 
         def below(quad, inner):
@@ -50,10 +56,23 @@
                 b[i] = right_row
             return inner
 
-        lax.fori_loop((base + step) // 4, NB // 4, below, 0)
-        return carry
-
-    lax.fori_loop(0, NB // step, block, 0)
+        lax.fori_loop((base + step) // 4, end // 4, below, 0)
+        return carry
+
+    group = 32
+    for start in range(0, NB, group):
+        end = start + group
+        lax.fori_loop(start // step, end // step, functools.partial(block, end=end), 0)
+        if end < NB:
+            for f in range(a.shape[1]):
+                left, right = a[start:end, f, :], b[start:end, f, :]
+                turned = left.T[end:]
+                a[end:, f, :] -= jnp.dot(
+                    turned, left, precision=lax.Precision.HIGHEST, preferred_element_type=jnp.float32
+                )
+                b[end:, f, :] -= jnp.dot(
+                    turned, right, precision=lax.Precision.HIGHEST, preferred_element_type=jnp.float32
+                )
 
 
 def factor_kernel(gram_ref, out_ref, a, b):
@@ -78,11 +97,207 @@
     )(gram)
 
 
+def panel_kernel(
+    peers, cols, lead_ref, target_ref, own_ref, out_ref,
+    got_lead, got_target, total, panel,
+    lead_send, lead_recv, target_send, target_recv, part_send, part_recv,
+    row_send, row_recv, pair_send, pair_recv, core_send, core_recv, home,
+):
+    me, col = lax.axis_index("rows"), lax.axis_index("cols")
+    pairs = cols // 2
+    core, pair = lax.rem(col, 2), lax.div(col, 2)
+    twin = pair * 2 + 1 - core
+    rows = own_ref.shape[0]
+    part = rows // cols
+    chunks = lead_ref.shape[1] // NB
+
+    def at(r, c):
+        return {"rows": r, "cols": c}
+
+    barrier = pltpu.get_barrier_semaphore()
+    for k in range(1, peers):
+        pl.semaphore_signal(barrier, inc=1, device_id=at(lax.rem(me + k, peers), col), device_id_type=MESH)
+    for k in range(1, cols):
+        pl.semaphore_signal(barrier, inc=1, device_id=at(me, lax.rem(col + k, cols)), device_id_type=MESH)
+    pl.semaphore_wait(barrier, peers + cols - 2)
+
+    def lead_copy(to, slot_from, slot):
+        return (
+            pltpu.make_async_remote_copy(
+                src_ref=lead_ref.at[slot_from], dst_ref=got_lead.at[slot],
+                send_sem=lead_send.at[slot_from], recv_sem=lead_recv.at[slot],
+                device_id=at(to, 0), device_id_type=MESH,
+            ),
+            pltpu.make_async_remote_copy(
+                src_ref=target_ref.at[slot_from], dst_ref=got_target.at[slot],
+                send_sem=target_send.at[slot_from], recv_sem=target_recv.at[slot],
+                device_id=at(to, 0), device_id_type=MESH,
+            ),
+        )
+
+    def part_copy(index):
+        where = pl.ds(pl.multiple_of(index * part, 16), part)
+        return pltpu.make_async_remote_copy(
+            src_ref=panel.at[where], dst_ref=panel.at[where],
+            send_sem=part_send.at[index], recv_sem=part_recv.at[index],
+            device_id=at(me, index), device_id_type=MESH,
+        )
+
+    def placed(target, lead):
+        ids = lax.broadcasted_iota(jnp.int32, (rows, NB), 0).astype(jnp.float32)
+        chosen = jnp.where(ids == target, 1.0, 0.0).astype(jnp.bfloat16)
+        return jnp.dot(chosen, lead, preferred_element_type=jnp.float32)
+
+    @pl.when(col == 0)
+    def _():
+        def send(k, carry):
+            to = lax.rem(me + k, peers)
+            for copy in lead_copy(to, to, me):
+                copy.start()
+            return carry
+
+        lax.fori_loop(1, peers, send, 0)
+        total[...] = own_ref[...].astype(jnp.float32)
+        for u in range(chunks):
+            total[...] += placed(target_ref[me, pl.ds(u, 1), :], lead_ref[me, pl.ds(u * NB, NB), :])
+
+        def take(k, carry):
+            source = lax.rem(me + peers - k, peers)
+            for copy in lead_copy(source, source, source):
+                copy.wait_recv()
+            for u in range(chunks):
+                total[...] += placed(got_target[source, pl.ds(u, 1), :], got_lead[source, pl.ds(u * NB, NB), :])
+            return carry
+
+        lax.fori_loop(1, peers, take, 0)
+        panel[...] = total[...].astype(jnp.bfloat16)
+        for index in range(1, cols):
+            part_copy(index).start()
+
+    @pl.when(col != 0)
+    def _():
+        part_copy(col).wait_recv()
+
+    mine = pl.ds(pl.multiple_of(col * part, 16), part)
+
+    def row_copy(k, source):
+        return pltpu.make_async_remote_copy(
+            src_ref=panel.at[mine], dst_ref=out_ref.at[source, mine],
+            send_sem=row_send.at[k], recv_sem=row_recv.at[source],
+            device_id=at(lax.rem(me + k, peers), col), device_id_type=MESH,
+        )
+
+    def pair_copy(source, k, owner):
+        where = pl.ds(pl.multiple_of((owner * 2 + core) * part, 16), part)
+        return pltpu.make_async_remote_copy(
+            src_ref=out_ref.at[source, where], dst_ref=out_ref.at[source, where],
+            send_sem=pair_send.at[source, k], recv_sem=pair_recv.at[source, owner],
+            device_id=at(me, lax.rem(pair + k, pairs) * 2 + core), device_id_type=MESH,
+        )
+
+    def core_copy(source, owner, side):
+        where = pl.ds(pl.multiple_of((owner * 2 + side) * part, 16), part)
+        return pltpu.make_async_remote_copy(
+            src_ref=out_ref.at[source, where], dst_ref=out_ref.at[source, where],
+            send_sem=core_send.at[source, owner], recv_sem=core_recv.at[source, owner],
+            device_id=at(me, twin), device_id_type=MESH,
+        )
+
+    def push(k, carry):
+        row_copy(k, me).start()
+        return carry
+
+    lax.fori_loop(1, peers, push, 0)
+    local = pltpu.make_async_copy(panel.at[mine], out_ref.at[me, mine], home)
+    local.start()
+    local.wait()
+
+    def relay(source):
+        for k in range(1, pairs):
+            pair_copy(source, k, pair).start()
+        core_copy(source, pair, core).start()
+
+    def onward(source):
+        for k in range(1, pairs):
+            owner = lax.rem(pair + k, pairs)
+            pair_copy(source, k, owner).wait_recv()
+            core_copy(source, owner, core).start()
+
+    relay(me)
+
+    def step(k, carry):
+        source = lax.rem(me + peers - k, peers)
+        row_copy(k, source).wait_recv()
+        relay(source)
+        onward(lax.rem(source + 1, peers))
+        return carry
+
+    lax.fori_loop(1, peers, step, 0)
+    onward(lax.rem(me + 1, peers))
+
+    def finish(source, carry):
+        for owner in range(pairs):
+            core_copy(source, owner, 1 - core).wait_recv()
+            core_copy(source, owner, core).wait_send()
+        for k in range(1, pairs):
+            pair_copy(source, k, pair).wait_send()
+        return carry
+
+    lax.fori_loop(0, peers, finish, 0)
+
+    def sent(k, carry):
+        row_copy(k, me).wait_send()
+        return carry
+
+    lax.fori_loop(1, peers, sent, 0)
+
+    @pl.when(col == 0)
+    def _():
+        def leads(k, carry):
+            to = lax.rem(me + k, peers)
+            for copy in lead_copy(to, to, me):
+                copy.wait_send()
+            return carry
+
+        lax.fori_loop(1, peers, leads, 0)
+        for index in range(1, cols):
+            part_copy(index).wait_send()
+
+
+def gather_panel(leads, targets, own):
+    peers, cols = lax.axis_size("rows"), lax.axis_size("cols")
+    pairs = cols // 2
+    vmem = pl.BlockSpec(memory_space=pltpu.VMEM)
+    dma = pltpu.SemaphoreType.DMA
+    return pl.pallas_call(
+        functools.partial(panel_kernel, peers, cols),
+        out_shape=jax.ShapeDtypeStruct((peers,) + own.shape, jnp.bfloat16),
+        in_specs=[vmem] * 3,
+        out_specs=pl.BlockSpec(memory_space=pl.ANY),
+        scratch_shapes=[
+            pltpu.VMEM(leads.shape, leads.dtype),
+            pltpu.VMEM(targets.shape, targets.dtype),
+            pltpu.VMEM(own.shape, jnp.float32),
+            pltpu.VMEM(own.shape, jnp.bfloat16),
+            dma((peers,)), dma((peers,)), dma((peers,)), dma((peers,)),
+            dma((cols,)), dma((cols,)),
+            dma((peers,)), dma((peers,)),
+            dma((peers, pairs)), dma((peers, pairs)),
+            dma((peers, pairs)), dma((peers, pairs)),
+            dma,
+        ],
+        compiler_params=pltpu.CompilerParams(
+            collective_id=0, has_side_effects=True, vmem_limit_bytes=40 << 20
+        ),
+        cost_estimate=pl.CostEstimate(flops=1 << 30, bytes_accessed=8 << 20, transcendentals=0),
+    )(leads, targets, own)
+
+
 def on_device(front_rows, heights, child_rows, child_dest, child_slot, parent_ids):
     fronts, height_cap, width = front_rows.shape
     peers = lax.axis_size("rows")
     count = child_rows.shape[0]
-    capacity = max(2, 2 * count // peers)
+    capacity = -(-max(2, 2 * count // peers) // NB) * NB
     slots = peers * capacity
     local_rows = fronts * height_cap
     destination = child_dest[:, 0]
@@ -97,25 +312,16 @@
     tags = jnp.stack([child_front, child_slot], axis=0).astype(jnp.bfloat16)
     send_tags = lax.dot_general(
         tags, packing, (((1,), (1,)), ((), ())), preferred_element_type=jnp.float32
-    ).astype(jnp.bfloat16)
-    tag_rows = -(-2 * capacity // NB)
-    send_tags = jnp.transpose(send_tags.reshape(2, peers, capacity), (1, 0, 2)).reshape(peers, 2 * capacity)
-    send_tags = jnp.pad(send_tags, ((0, 0), (0, tag_rows * NB - 2 * capacity))).reshape(peers, tag_rows, NB)
-    sent = jnp.concatenate([send_lead.reshape(peers, capacity, NB), send_tags], axis=1)
-    got = lax.all_to_all(sent, "rows", split_axis=0, concat_axis=0, tiled=True)
-    got_lead = got[:, :capacity].reshape(slots, NB)
-    got_tags = got[:, capacity:].reshape(peers, tag_rows * NB)[:, : 2 * capacity].astype(jnp.int32)
-    got_tags = got_tags.reshape(peers, 2, capacity)
-    target = (got_tags[:, 0] * height_cap + got_tags[:, 1]).reshape(slots)
-    placing = (jnp.arange(local_rows, dtype=jnp.int32)[:, None] == target[None, :]).astype(jnp.bfloat16)
-    added = jnp.dot(placing, got_lead, preferred_element_type=jnp.float32)
+    )
+    targets = (send_tags[0] * height_cap + send_tags[1]).reshape(peers, capacity // NB, NB)
+    targets = jnp.pad(targets, ((0, 0), (0, -(capacity // NB) % 8), (0, 0)))
     live_mask = jnp.arange(height_cap, dtype=jnp.int32)[None, :] < heights[0][:, None]
     own = jnp.where(live_mask[:, :, None], front_rows, jnp.zeros_like(front_rows))
-    panel_own = (own[:, :, :NB].reshape(local_rows, NB).astype(jnp.float32) + added).astype(jnp.bfloat16)
-    panel_own = lax.psum(
-        jnp.where(lax.axis_index("cols") == 0, panel_own, jnp.zeros_like(panel_own)), "cols"
-    )
-    panel_all = lax.all_gather(panel_own, "rows", axis=0, tiled=True)
+    gathered = gather_panel(
+        send_lead.reshape(peers, capacity, NB), targets, own[:, :, :NB].reshape(local_rows, NB)
+    )
+    panel_own = lax.dynamic_index_in_dim(gathered, lax.axis_index("rows"), 0, keepdims=False)
+    panel_all = gathered.reshape(peers * local_rows, NB)
     by_front = panel_all.reshape(peers, fronts, height_cap, NB)
     gram = jnp.einsum("pfhk,pfhj->fkj", by_front, by_front, preferred_element_type=jnp.float32)
     key = destination * local_rows + child_front * height_cap + child_slot
@@ -127,12 +333,13 @@
     local = local + jnp.einsum(
         "fhk,fhc->fkc", panel_own.reshape(fronts, height_cap, NB), own, preferred_element_type=jnp.float32
     )
-    columns = lax.psum_scatter(
-        jnp.transpose(local.reshape(fronts, NB, peers, width // peers), (2, 0, 1, 3)),
-        "rows",
-        scatter_dimension=0,
-        tiled=True,
-    )[0]
+    norm = jnp.sqrt(jnp.diagonal(gram, axis1=1, axis2=2))
+    reach = LARGEST * math.sqrt(height_cap + count) * math.sqrt(2 * count // peers + 2)
+    scale = norm * (reach / 60000.0)
+    local = local * (1.0 / scale)[:, :, None]
+    parts = jnp.transpose(local.reshape(fronts, NB, peers, width // peers), (2, 0, 1, 3)).astype(jnp.float16)
+    parts = lax.all_to_all(parts, "rows", split_axis=0, concat_axis=0, tiled=True)
+    columns = jnp.sum(parts.astype(jnp.float32), axis=0) * scale[:, :, None]
     inverse = factor(gram)
     return jnp.einsum(
         "fij,fjc->fic", inverse, columns, precision=lax.Precision.HIGHEST, preferred_element_type=jnp.float32

time: 233 us -> 127 us (0.55)
  waiting for transfers between devices: 135 us -> 27.9 us
  Pallas kernels: 44.3 us -> 60.5 us
  between operations: 13.3 us -> 0.17 us
  local copies, waits for them, and re-layouts: 3.65 us -> 10.8 us
  matrix products: 24.7 us -> 18.1 us
    all_gather x1 -> x0, waiting for transfers between devices: 51.4 us -> none  [on_device(): panel_all = lax.all_gather(panel_own, 'rows', axis=0, tiled=True)]
    pallas_call x0 -> x1, Pallas kernels: none -> 39.7 us  [gather_panel(): pl.pallas_call(functools.partial(panel_kernel, peers, cols), out_shape=ja...]
    reduce_scatter x1 -> x0, waiting for transfers between devices: 39.6 us -> none  [on_device(): lax.psum_scatter(jnp.transpose(local.reshape(fronts, NB, peers, width //...]
    psum x1 -> x0, waiting for transfers between devices: 31.2 us -> none  [on_device(): lax.psum(jnp.where(lax.axis_index('cols') == 0, panel_own, jnp.zeros_like...]
    pallas_call x1, Pallas kernels: 44.3 us -> 20.8 us  [factor(): pl.pallas_call(factor_kernel, out_shape=jax.ShapeDtypeStruct(gram.shape,...]
    all_to_all x1, waiting for transfers between devices: 12.8 us -> 27.9 us  [on_device(): lax.all_to_all(parts, 'rows', split_axis=0, concat_axis=0, tiled=True)]
    dot_general x0 -> x1, local copies, waits for them, and re-layouts: none -> 4.58 us  [on_device(): jnp.einsum('pfhk,pfhj->fkj', by_front, by_front, preferred_element_type=j...]
    dot_general x1, matrix products: 8.56 us -> 5.51 us  [on_device(): jnp.dot(choosing, panel_all, preferred_element_type=jnp.float32)]
  transfers between devices with their start and end apart: 4 -> 1, of which waited for: 4 -> 1; matrix products, arithmetic and copies ran while one was open for 2% -> 0% of each run, Pallas kernels for 19% -> 16%
where the time goes in v2:
time: 127 us
  Pallas kernels  60.5 us (48%)
  waiting for transfers between devices  27.9 us (22%)
  matrix products  18.1 us (14%)
  local copies, waits for them, and re-layouts  10.8 us (9%)
  starting transfers between devices  7.28 us (6%)
  other arithmetic  2.22 us (2%)
    pallas_call x1, Pallas kernels, gather_panel(): pl.pallas_call(functools.partial(panel_kernel, peers, cols), out_shape=ja...  39.7 us
    all_to_all x1, waiting for transfers between devices, on_device(): lax.all_to_all(parts, 'rows', split_axis=0, concat_axis=0, tiled=True)  27.9 us
    pallas_call x1, Pallas kernels, factor(): pl.pallas_call(factor_kernel, out_shape=jax.ShapeDtypeStruct(gram.shape,...  20.8 us
    all_to_all x1, starting transfers between devices, on_device(): lax.all_to_all(parts, 'rows', split_axis=0, concat_axis=0, tiled=True)  7.28 us
    dot_general x1, matrix products, on_device(): jnp.dot(choosing, panel_all, preferred_element_type=jnp.float32)  5.51 us
    dot_general x1, local copies, waits for them, and re-layouts, on_device(): jnp.einsum('pfhk,pfhj->fkj', by_front, by_front, preferred_element_type=j...  4.58 us
    dot_general x1, matrix products, on_device(): jnp.einsum('fsk,sc->fkc', picked, child_rows, preferred_element_type=jnp....  4.07 us
  transfers between devices with their start and end apart: 1, of which 1 were waited for; matrix products, arithmetic and copies ran while one was open for 0% of the time, Pallas kernels for 16%

profile of v2, /device:TPU:0, one launch (start us, length us, event | category | flops | bytes accessed | tf_op | source)
XLA Modules:
  0.0 126.9 jit_solution(10932200185798259806)
XLA Ops:
  0.0 0.7 convert.9
  0.7 0.7 broadcast_in_dim.19
  1.4 0.1 eq.65
  1.5 1.2 fusion.14
  2.7 0.8 add_add_fusion
  3.5 0.1 broadcast_in_dim.16
  3.6 0.1 stack_reshape.4
  3.7 2.5 %fusion.7 = bf16[2048,128]{1,0:T(8,128)(2,1)S(1)} fusion(s32[1024]{0:T(1024)S(1)} %get-tuple-element.6, bf16[1024,1024]{1,0:T(8,128)(2,1)} %param.8), kind=kOutput, calls=%fused_computation.13 | convolution fusion | flops 539230208 | bytes 790528 | tf_op jit(solution)/shard_map/dot_general | solution.py:311
  6.1 0.0 copy-start.3
  6.2 0.0 copy-start.2
  6.2 1.5 %fusion.2 = f32[2,2048]{1,0:T(2,128)S(1)} fusion(s32[1024]{0:T(1024)S(1)} %get-tuple-element.6, bf16[1,1024]{1,0:T(2,128)(2,1)S(1)} %stack.8, bf16[1,1024]{1,0:T(2,128)(2,1)S(1)} %stack_reshape.4), kind=kOutput, calls=%fused_computation.5 | convolution fusion | flops 10493952 | bytes 24576 | tf_op jit(solution)/shard_map/dot_general | solution.py:313
  7.7 0.0 copy-done.3
  7.7 0.1 iota_compare_fusion.18
  7.7 0.0 copy-done.2
  7.8 0.2 broadcast_select_fusion
  8.0 0.0 copy-start
  8.0 0.1 slice.20
  8.1 1.3 %copy-done = bf16[8,128,1024]{2,1,0:T(8,128)(2,1)} copy-done((bf16[8,128,1024]{2,1,0:T(8,128)(2,1)}, bf16[8,128,1024]{2,1,0:T(8,128)(2,1)S(1)}, u32[]{:S(2)}) %copy-start) | copy-done | bytes 2097176
  9.4 39.7 %shard_map.64 = bf16[8,1024,128]{2,1,0:T(8,128)(2,1)S(1)} custom-call(bf16[8,256,128]{2,1,0:T(8,128)(2,1)S(1)} %bitcast.36, f32[8,8,128]{2,1,0:T(8,128)S(1)} %pad.4.target_ref, bf16[1024,128]{1,0:T(8,128)(2,1)S(1)} %bitcast.35), custom_call_target="tpu_custom_call" | custom-call | flops 1073741824 | bytes 8388608 | tf_op jit(solution)/shard_map/pallas_call | solution.py:272
  49.1 0.8 convolution_bitcast_fusion.gram_ref
  49.8 4.6 %copy.28 = f32[8,128,128]{0,2,1:T(8,128)} copy(f32[8,128,128]{2,1,0:T(8,128)S(1)} %convolution_bitcast_fusion.gram_ref) | data formatting | bytes 1048576 | tf_op jit(solution)/shard_map/pfhk,pfhj->fkj/dot_general | solution.py:326
  54.4 1.8 %gather_fusion = f32[128,8]{1,0:T(8,128)S(1)} fusion(f32[8,128,128]{0,2,1:T(8,128)} %copy.28, s32[128]{0:T(128)S(1)} %or_bitcast_fusion), kind=kCustom, calls=%fused_computation | custom fusion | bytes 9216 | tf_op jit(solution)/shard_map/jit(diagonal)/gather | solution.py:336
  56.3 5.5 %fusion.12 = bf16[1024,128]{1,0:T(8,128)(2,1)S(1)} fusion(bf16[8192,128]{1,0:T(8,128)(2,1)S(1)} %bitcast.34, s32[1024]{0:T(1024)S(1)} %get-tuple-element.5), kind=kOutput, calls=%fused_computation.21 | convolution fusion | flops 2156003328 | bytes 2363392 | tf_op jit(solution)/shard_map/dot_general | solution.py:329
  61.8 0.1 copy.26
  62.0 0.0 copy-start.1
  62.0 4.1 %fusion.8 = f32[8,128,1024]{2,1,0:T(8,128)S(1)} fusion(bf16[1024,1024]{1,0:T(8,128)(2,1)} %param.8, bf16[1024,128]{0,1:T(8,128)(2,1)S(1)} %copy.26, bf16[8,1024]{1,0:T(8,128)(2,1)S(1)} %fusion.22), kind=kOutput, calls=%fused_computation.15 | convolution fusion | flops 2148532224 | bytes 6569984 | tf_op jit(solution)/shard_map/fsk,sc->fkc/dot_general | solution.py:332
  66.0 0.0 copy-done.1
  66.1 1.0 fusion.11
  67.1 1.9 %copy.35 = f16[8,16,8,8,128]{4,3,1,0,2:T(8,128)(2,1)} copy(f16[8,16,8,8,128]{4,3,2,1,0:T(8,128)(2,1)S(1)} %fusion.11) | data formatting | bytes 4194304 | tf_op jit(solution)/shard_map/convert_element_type | solution.py:340
  69.0 7.3 %all-to-all-start = ((f16[8,8,128,128]{3,2,1,0:T(8,128)(2,1)}), f16[8,8,128,128]{3,2,1,0:T(8,128)(2,1)S(1)}, u32[]{:S(2)}, u32[]{:S(2)}) async-start(f16[8,8,128,128]{3,2,1,0:T(8,128)(2,1)} %bitcast.37), calls=%async_computation | async-start | bytes 4194304 | tf_op jit(solution)/shard_map/all_to_all | solution.py:341
  76.3 20.8 %shard_map.65 = f32[8,128,128]{2,1,0:T(8,128)S(1)} custom-call(f32[8,128,128]{2,1,0:T(8,128)S(1)} %convolution_bitcast_fusion.gram_ref), custom_call_target="tpu_custom_call" | custom-call | flops 40000000000 | bytes 1048576 | tf_op jit(solution)/shard_map/pallas_call | solution.py:89
  97.0 27.9 %all-to-all-done = f16[8,8,128,128]{3,2,1,0:T(8,128)(2,1)S(1)} async-done(((f16[8,8,128,128]{3,2,1,0:T(8,128)(2,1)}), f16[8,8,128,128]{3,2,1,0:T(8,128)(2,1)S(1)}, u32[]{:S(2)}, u32[]{:S(2)}) %all-to-all-start) | async-done | bytes 2097184 | tf_op jit(solution)/shard_map/all_to_all | solution.py:341
  124.9 0.5 convert_reduce_fusion
  125.4 1.5 %fusion.17 = f32[8,128,128]{2,1,0:T(8,128)} fusion(f32[8,128,128]{2,1,0:T(8,128)S(1)} %shard_map.65, f32[8,128,128]{2,1,0:T(8,128)S(1)} %convert_reduce_fusion, f32[8,128]{1,0:T(8,128)S(1)} %multiply_bitcast_fusion), kind=kOutput, calls=%fused_computation.26 | convolution fusion | flops 201457664 | bytes 1576960 | tf_op jit(solution)/shard_map/fij,fjc->fic/dot_general | solution.py:344
  (9 shorter events, 0.1 us)
Async XLA Ops:
  6.1 1.5 %copy-start.3 = (s32[1,8]{1,0:T(1,128)S(1)}, s32[1,8]{1,0:T(1,128)}, u32[]{:S(2)}) copy-start(s32[1,8]{1,0:T(1,128)} %param.7) | copy-start | bytes 100
  6.2 1.6 %copy-start.2 = (bf16[8,128,1024]{2,1,0:T(8,128)(2,1)S(1)}, bf16[8,128,1024]{2,1,0:T(8,128)(2,1)}, u32[]{:S(2)}) copy-start(bf16[8,128,1024]{2,1,0:T(8,128)(2,1)} %param.6) | copy-start | bytes 6291460
  8.0 1.4 %copy-start = (bf16[8,128,1024]{2,1,0:T(8,128)(2,1)}, bf16[8,128,1024]{2,1,0:T(8,128)(2,1)S(1)}, u32[]{:S(2)}) copy-start(bf16[8,128,1024]{2,1,0:T(8,128)(2,1)S(1)} %broadcast_select_fusion) | copy-start | bytes 6291460
  62.0 4.1 %copy-start.1 = (bf16[8,128,1024]{2,1,0:T(8,128)(2,1)S(1)}, bf16[8,128,1024]{2,1,0:T(8,128)(2,1)}, u32[]{:S(2)}) copy-start(bf16[8,128,1024]{2,1,0:T(8,128)(2,1)} %copy-done) | copy-start | bytes 6291460
  69.0 56.0 %all-to-all-start = ((f16[8,8,128,128]{3,2,1,0:T(8,128)(2,1)}), f16[8,8,128,128]{3,2,1,0:T(8,128)(2,1)S(1)}, u32[]{:S(2)}, u32[]{:S(2)}) async-start(f16[8,8,128,128]{3,2,1,0:T(8,128)(2,1)} %bitcast.37), calls=%async_computation | async-start | bytes 4194304 | tf_op jit(solution)/shard_map/all_to_all | solution.py:341

commit v3 on v2

--- a/solution.py
+++ b/solution.py
@@ -144,9 +144,12 @@
         )
 
     def placed(target, lead):
-        ids = lax.broadcasted_iota(jnp.int32, (rows, NB), 0).astype(jnp.float32)
+        ids = lax.broadcasted_iota(jnp.int32, (rows, target.shape[1]), 0).astype(jnp.float32)
         chosen = jnp.where(ids == target, 1.0, 0.0).astype(jnp.bfloat16)
         return jnp.dot(chosen, lead, preferred_element_type=jnp.float32)
+
+    def spread(ref, source):
+        return jnp.concatenate([ref[source, pl.ds(u, 1), :] for u in range(chunks)], axis=1)
 
     @pl.when(col == 0)
     def _():
@@ -158,20 +161,18 @@
 
         lax.fori_loop(1, peers, send, 0)
         total[...] = own_ref[...].astype(jnp.float32)
-        for u in range(chunks):
-            total[...] += placed(target_ref[me, pl.ds(u, 1), :], lead_ref[me, pl.ds(u * NB, NB), :])
+        total[...] += placed(spread(target_ref, me), lead_ref[me])
 
         def take(k, carry):
             source = lax.rem(me + peers - k, peers)
             for copy in lead_copy(source, source, source):
                 copy.wait_recv()
-            for u in range(chunks):
-                total[...] += placed(got_target[source, pl.ds(u, 1), :], got_lead[source, pl.ds(u * NB, NB), :])
+            total[...] += placed(spread(got_target, source), got_lead[source])
             return carry
 
         lax.fori_loop(1, peers, take, 0)
         panel[...] = total[...].astype(jnp.bfloat16)
-        for index in range(1, cols):
+        for index in range(cols - 1, 0, -1):
             part_copy(index).start()
 
     @pl.when(col != 0)
@@ -333,7 +334,7 @@
     local = local + jnp.einsum(
         "fhk,fhc->fkc", panel_own.reshape(fronts, height_cap, NB), own, preferred_element_type=jnp.float32
     )
-    norm = jnp.sqrt(jnp.diagonal(gram, axis1=1, axis2=2))
+    norm = jnp.sqrt(jnp.sum(jnp.where(jnp.eye(NB, dtype=bool)[None], gram, 0.0), axis=1))
     reach = LARGEST * math.sqrt(height_cap + count) * math.sqrt(2 * count // peers + 2)
     scale = norm * (reach / 60000.0)
     local = local * (1.0 / scale)[:, :, None]

time: 127 us -> 122 us (0.961)
  local copies, waits for them, and re-layouts: 10.8 us -> 5.13 us
  other arithmetic: 2.22 us -> 4.51 us
  matrix products: 18.1 us -> 16.5 us
  starting transfers between devices: 7.28 us -> 5.7 us
  Pallas kernels: 60.5 us -> 61.8 us
    dot_general x1 -> x0, local copies, waits for them, and re-layouts: 4.58 us -> none  [on_device(): jnp.einsum('pfhk,pfhj->fkj', by_front, by_front, preferred_element_type=j...]
    gather x2 -> x0, local copies, waits for them, and re-layouts: 1.81 us -> none  [on_device(): norm = jnp.sqrt(jnp.diagonal(gram, axis1=1, axis2=2))]
    dot_general x1, matrix products: 4.07 us -> 2.34 us  [on_device(): jnp.einsum('fsk,sc->fkc', picked, child_rows, preferred_element_type=jnp....]
    reduce_sum x1, other arithmetic: 0.46 us -> 2.09 us  [on_device(): columns = jnp.sum(parts.astype(jnp.float32), axis=0) * scale[:, :, None]]
    all_to_all x1, starting transfers between devices: 7.28 us -> 5.7 us  [on_device(): lax.all_to_all(parts, 'rows', split_axis=0, concat_axis=0, tiled=True)]
    pallas_call x1, Pallas kernels: 39.7 us -> 41.1 us  [gather_panel(): pl.pallas_call(functools.partial(panel_kernel, peers, cols), out_shape=ja...]
  transfers between devices with their start and end apart: 1 -> 1, of which waited for: 1 -> 1; matrix products, arithmetic and copies ran while one was open for 0% -> 0% of each run, Pallas kernels for 16% -> 17%
where the time goes in v3:
time: 122 us
  Pallas kernels  61.8 us (51%)
  waiting for transfers between devices  28 us (23%)
  matrix products  16.5 us (14%)
  starting transfers between devices  5.7 us (5%)
  local copies, waits for them, and re-layouts  5.13 us (4%)
  other arithmetic  4.51 us (4%)
    pallas_call x1, Pallas kernels, gather_panel(): pl.pallas_call(functools.partial(panel_kernel, peers, cols), out_shape=ja...  41.1 us
    all_to_all x1, waiting for transfers between devices, on_device(): lax.all_to_all(parts, 'rows', split_axis=0, concat_axis=0, tiled=True)  28 us
    pallas_call x1, Pallas kernels, factor(): pl.pallas_call(factor_kernel, out_shape=jax.ShapeDtypeStruct(gram.shape,...  20.7 us
    all_to_all x1, starting transfers between devices, on_device(): lax.all_to_all(parts, 'rows', split_axis=0, concat_axis=0, tiled=True)  5.7 us
    dot_general x1, matrix products, on_device(): jnp.dot(choosing, panel_all, preferred_element_type=jnp.float32)  5.48 us
    dot_general x1, matrix products, on_device(): jnp.dot(packing, child_rows[:, :NB], preferred_element_type=jnp.float32)  2.63 us
  transfers between devices with their start and end apart: 1, of which 1 were waited for; matrix products, arithmetic and copies ran while one was open for 0% of the time, Pallas kernels for 17%

profile of v3, /device:TPU:0, one launch (start us, length us, event | category | flops | bytes accessed | tf_op | source)
XLA Modules:
  0.0 121.8 jit_solution(8077657354509978149)
XLA Ops:
  0.0 0.7 convert.9
  0.7 0.7 iota_compare_fusion.19
  1.4 0.1 broadcast_in_dim.22
  1.5 0.1 stack_reshape.4
  1.6 1.2 %fusion.14 = f32[1024]{0:T(1024)S(1)} fusion(s32[1024]{0:T(1024)} %bitcast.33), kind=kOutput, calls=%fused_computation.22 | convolution fusion | flops 17873920 | bytes 8192 | tf_op jit(solution)/shard_map/dot_general | solution.py:308
  2.8 0.7 broadcast_in_dim.29
  3.5 0.1 eq.72
  3.6 0.8 add_add_fusion
  4.4 1.5 %fusion.2 = f32[2,2048]{1,0:T(2,128)S(1)} fusion(s32[1024]{0:T(1024)S(1)} %get-tuple-element.8, bf16[1,1024]{1,0:T(2,128)(2,1)S(1)} %stack.8, bf16[1,1024]{1,0:T(2,128)(2,1)S(1)} %stack_reshape.4), kind=kOutput, calls=%fused_computation.4 | convolution fusion | flops 10493952 | bytes 24576 | tf_op jit(solution)/shard_map/dot_general | solution.py:314
  5.9 0.0 copy-start.2
  5.9 2.6 %fusion.7 = bf16[2048,128]{1,0:T(8,128)(2,1)S(1)} fusion(s32[1024]{0:T(1024)S(1)} %get-tuple-element.8, bf16[1024,1024]{1,0:T(8,128)(2,1)} %param.8), kind=kOutput, calls=%fused_computation.12 | convolution fusion | flops 539230208 | bytes 790528 | tf_op jit(solution)/shard_map/dot_general | solution.py:312
  8.5 0.0 copy-done.2
  8.5 0.2 broadcast_select_fusion
  8.8 0.0 copy-start
  8.8 0.1 slice.18
  8.9 1.2 %copy-done = bf16[8,128,1024]{2,1,0:T(8,128)(2,1)} copy-done((bf16[8,128,1024]{2,1,0:T(8,128)(2,1)}, bf16[8,128,1024]{2,1,0:T(8,128)(2,1)S(1)}, u32[]{:S(2)}) %copy-start) | copy-done | bytes 2097176
  10.1 41.1 %shard_map.64 = bf16[8,1024,128]{2,1,0:T(8,128)(2,1)S(1)} custom-call(bf16[8,256,128]{2,1,0:T(8,128)(2,1)S(1)} %bitcast.30, f32[8,8,128]{2,1,0:T(8,128)S(1)} %pad.4.target_ref, bf16[1024,128]{1,0:T(8,128)(2,1)S(1)} %bitcast.29), custom_call_target="tpu_custom_call" | custom-call | flops 1073741824 | bytes 8388608 | tf_op jit(solution)/shard_map/pallas_call | solution.py:273
  51.2 5.5 %fusion.12 = bf16[1024,128]{1,0:T(8,128)(2,1)S(1)} fusion(bf16[8192,128]{1,0:T(8,128)(2,1)S(1)} %bitcast.27, s32[1024]{0:T(1024)S(1)} %get-tuple-element.7), kind=kOutput, calls=%fused_computation.20 | convolution fusion | flops 2156003328 | bytes 2363392 | tf_op jit(solution)/shard_map/dot_general | solution.py:330
  56.7 0.1 copy.13
  56.9 0.0 copy-start.3
  56.9 0.8 select_reduce_fusion
  57.7 0.8 copy-done.3
  58.5 0.0 copy-start.1
  58.5 2.3 %fusion.8 = f32[8,128,1024]{2,1,0:T(8,128)S(1)} fusion(bf16[1024,1024]{1,0:T(8,128)(2,1)S(1)} %copy-done.3, bf16[1024,128]{0,1:T(8,128)(2,1)S(1)} %copy.13, bf16[8,1024]{1,0:T(8,128)(2,1)S(1)} %fusion.22), kind=kOutput, calls=%fused_computation.14 | convolution fusion | flops 2148532224 | bytes 6569984 | tf_op jit(solution)/shard_map/fsk,sc->fkc/dot_general | solution.py:333
  60.8 0.0 copy-done.1
  60.8 1.0 fusion.11
  61.8 1.9 %copy.20 = f16[8,16,8,8,128]{4,3,1,0,2:T(8,128)(2,1)} copy(f16[8,16,8,8,128]{4,3,2,1,0:T(8,128)(2,1)S(1)} %fusion.11) | data formatting | bytes 4194304 | tf_op jit(solution)/shard_map/convert_element_type | solution.py:341
  63.7 5.7 %all-to-all-start = ((f16[8,8,128,128]{3,2,1,0:T(8,128)(2,1)}), f16[8,8,128,128]{3,2,1,0:T(8,128)(2,1)}, u32[]{:S(2)}, u32[]{:S(2)}) async-start(f16[8,8,128,128]{3,2,1,0:T(8,128)(2,1)} %bitcast.26), calls=%async_computation | async-start | bytes 4194304 | tf_op jit(solution)/shard_map/all_to_all | solution.py:342
  69.4 20.7 %shard_map.65 = f32[8,128,128]{2,1,0:T(8,128)S(1)} custom-call(f32[8,128,128]{2,1,0:T(8,128)S(1)} %get-tuple-element.11.gram_ref), custom_call_target="tpu_custom_call" | custom-call | flops 40000000000 | bytes 1048576 | tf_op jit(solution)/shard_map/pallas_call | solution.py:89
  90.1 28.0 %all-to-all-done = f16[8,8,128,128]{3,2,1,0:T(8,128)(2,1)} async-done(((f16[8,8,128,128]{3,2,1,0:T(8,128)(2,1)}), f16[8,8,128,128]{3,2,1,0:T(8,128)(2,1)}, u32[]{:S(2)}, u32[]{:S(2)}) %all-to-all-start) | async-done | bytes 2097184 | tf_op jit(solution)/shard_map/all_to_all | solution.py:342
  118.2 2.1 %convert_reduce_fusion = f32[8,128,128]{2,1,0:T(8,128)S(1)} fusion(f16[8,8,128,128]{3,2,1,0:T(8,128)(2,1)} %all-to-all-done), kind=kLoop, calls=%fused_computation.6 | loop fusion | flops 1966080 | bytes 2621440 | tf_op jit(solution)/shard_map/reduce_sum | solution.py:343
  120.3 1.5 %fusion.17 = f32[8,128,128]{2,1,0:T(8,128)} fusion(f32[8,128,128]{2,1,0:T(8,128)S(1)} %shard_map.65, f32[8,128,128]{2,1,0:T(8,128)S(1)} %convert_reduce_fusion, f32[8,128]{1,0:T(8,128)S(1)} %get-tuple-element.5), kind=kOutput, calls=%fused_computation.25 | convolution fusion | flops 201457664 | bytes 1576960 | tf_op jit(solution)/shard_map/fij,fjc->fic/dot_general | solution.py:345
  (7 shorter events, 0.1 us)
Async XLA Ops:
  5.9 2.6 %copy-start.2 = (bf16[8,128,1024]{2,1,0:T(8,128)(2,1)S(1)}, bf16[8,128,1024]{2,1,0:T(8,128)(2,1)}, u32[]{:S(2)}) copy-start(bf16[8,128,1024]{2,1,0:T(8,128)(2,1)} %param.6) | copy-start | bytes 6291460
  8.8 1.3 %copy-start = (bf16[8,128,1024]{2,1,0:T(8,128)(2,1)}, bf16[8,128,1024]{2,1,0:T(8,128)(2,1)S(1)}, u32[]{:S(2)}) copy-start(bf16[8,128,1024]{2,1,0:T(8,128)(2,1)S(1)} %broadcast_select_fusion) | copy-start | bytes 6291460
  56.9 1.6 %copy-start.3 = (bf16[1024,1024]{1,0:T(8,128)(2,1)S(1)}, bf16[1024,1024]{1,0:T(8,128)(2,1)}, u32[]{:S(2)}) copy-start(bf16[1024,1024]{1,0:T(8,128)(2,1)} %param.8) | copy-start | bytes 6291460
  58.5 2.3 %copy-start.1 = (bf16[8,128,1024]{2,1,0:T(8,128)(2,1)S(1)}, bf16[8,128,1024]{2,1,0:T(8,128)(2,1)}, u32[]{:S(2)}) copy-start(bf16[8,128,1024]{2,1,0:T(8,128)(2,1)} %copy-done) | copy-start | bytes 6291460
  63.7 54.5 %all-to-all-start = ((f16[8,8,128,128]{3,2,1,0:T(8,128)(2,1)}), f16[8,8,128,128]{3,2,1,0:T(8,128)(2,1)}, u32[]{:S(2)}, u32[]{:S(2)}) async-start(f16[8,8,128,128]{3,2,1,0:T(8,128)(2,1)} %bitcast.26), calls=%async_computation | async-start | bytes 4194304 | tf_op jit(solution)/shard_map/all_to_all | solution.py:342
